TPU v7x, 512 devices: a whole 4x4x16 slice. The times are simulated.
512 devices in a mesh: zone: 32 (over z, x_hi), freq: 16 (over x_lo, y, core).
Axes of the slice: x: 4 (x_hi: 2, x_lo: 2; x = x_hi * 2 + x_lo), y: 4, z: 16, core: 2. Of those that a mesh axis runs over, the one named last changes fastest.
Arguments:
- modulus: float32 [256, 3, 1, 1024], P('zone'), may hold values from 0.3 to 1.5
- first_moment: float32 [256, 3, 1, 1024], P('zone'), may hold values from -6 to 6
- second_moment: float32 [256, 3, 1, 1024], P('zone'), may hold values from 0.5 to 4
- fiber: float32 [256, 1, 1024], P('zone'), may hold values from -1 to 1
- measured: float32 [16, 128, 2, 8, 1024], P('freq', 'zone'), may hold values from -6 to 6
- wave_sq: float32 [16], P('freq'), may hold values from 0.5 to 5
- send_list: int32 [32, 32, 2], P('zone'), may hold values from -1 to 7, as said below
- brick_list: int32 [128, 8], P('zone'), may hold values from 0 to 63, as said below
Outputs:
- new_modulus: float32 [256, 3, 1, 1024], P('zone')
- new_first: float32 [256, 3, 1, 1024], P('zone')
- new_second: float32 [256, 3, 1, 1024], P('zone')
Inputs may be any that keep to these rules, and one draw needn't show every extreme that they name: `send_list`: entries are -1 or distinct local brick indices; for each owner and zone group the live slots are c < some count of 0 to 2, and owner o sends 2 bricks to group (o + 1) % 32. `brick_list`: every entry names a live slot of its zone group.
All inputs are finite; a program needn't handle non-finite values.
Results may differ from a plain program's by a relative error of at most 0.0001.
Values sent between devices are 32-bit elements; how exact they have to be, the bound alone decides.
A program may use at most 64 MiB of HBM per device.

v0:
```python
import jax
import jax.numpy as jnp
from jax import lax
from jax.sharding import PartitionSpec as P

BY = 32
BZ = 32
K = 8
SWEEPS = 6
relax_rate = 0.25
learn_rate = 0.1
beta_first = 0.9
beta_second = 0.99
smooth_rate = 0.5
adam_eps = 1e-08


def beside_sum(cube):
    padded = jnp.pad(cube, ((0, 0), (1, 1), (1, 1), (1, 1)))
    total = padded[:, 2:, 1:-1, 1:-1] + padded[:, :-2, 1:-1, 1:-1]
    total = total + padded[:, 1:-1, 2:, 1:-1] + padded[:, 1:-1, :-2, 1:-1]
    return total + padded[:, 1:-1, 1:-1, 2:] + padded[:, 1:-1, 1:-1, :-2]


def misfit(moduli, fiber_tile, observed, wave_value):
    shear = (moduli[0] + (moduli[1] - moduli[0]) * fiber_tile * fiber_tile).reshape(-1, BY, BZ)
    damping = moduli[2].reshape(-1, BY, BZ)
    diagonal_term = 6.0 * shear + wave_value
    start_field = observed.reshape(2, -1, BY, BZ)
    field = start_field
    for sweep_index in range(SWEEPS):
        stencil = 6.0 * field - beside_sum(field)
        resid_real = shear * (stencil[0] - damping * stencil[1]) - wave_value * field[0]
        resid_imag = shear * (stencil[1] + damping * stencil[0]) - wave_value * field[1]
        field = field - relax_rate * jnp.stack([resid_real, resid_imag]) / diagonal_term
    gap = field - start_field
    return jnp.sum(gap * gap)


def update(moduli, first_moment, second_moment, fiber_tile, descent):
    new_first = beta_first * first_moment + (1.0 - beta_first) * descent
    new_second = beta_second * second_moment + (1.0 - beta_second) * descent * descent
    stepped = moduli - learn_rate * new_first / (jnp.sqrt(new_second) + adam_eps)
    shaped = stepped.reshape(stepped.shape[:-1] + (-1, BZ))
    lower_cell = jnp.concatenate([shaped[..., :1], shaped[..., :-1]], axis=-1).reshape(
        stepped.shape
    )
    upper_cell = jnp.concatenate([shaped[..., 1:], shaped[..., -1:]], axis=-1).reshape(
        stepped.shape
    )
    weight = smooth_rate * (fiber_tile * fiber_tile)[:, None]
    smoothed = stepped + weight * (0.5 * (lower_cell + upper_cell) - stepped)
    return (smoothed, new_first, new_second)


def to_owned(returned, owner_pick):
    flattened = returned.reshape(owner_pick.shape[1], -1)
    return jnp.dot(owner_pick, flattened, precision=lax.Precision.HIGHEST)


def on_device(
    modulus, first_moment, second_moment, fiber, measured, wave_sq, send_list, brick_list
):
    zone_count = lax.axis_size("zone")
    freq_count = lax.axis_size("freq")
    owned_count = modulus.shape[0]
    rows_brick = modulus.shape[2]
    depth = modulus.shape[3]
    slot_cap = send_list.shape[2]
    owner_list = send_list[0]
    live_mask = owner_list >= 0
    safe_ids = jnp.where(live_mask, owner_list, 0)
    stacked = jnp.concatenate([modulus, fiber[:, None]], axis=1)
    outgoing = jnp.where(live_mask[:, :, None, None, None], stacked[safe_ids], 0.0)
    arrived = lax.all_to_all(outgoing, "zone", split_axis=0, concat_axis=0, tiled=True)
    slot_data = arrived.reshape(zone_count * slot_cap, 4, rows_brick, depth)
    wave_value = wave_sq[0]

    def solve(subzone_item):
        brick_ids, observed = subzone_item
        picked_rows = slot_data[brick_ids]
        subzone_par = jnp.swapaxes(picked_rows, 0, 1).reshape(4, K * rows_brick, depth)
        gradient = jax.grad(misfit)(subzone_par[:3], subzone_par[3], observed, wave_value)
        return jnp.swapaxes(gradient.reshape(3, K, rows_brick, depth), 0, 1)

    gradients = lax.map(solve, (brick_list, measured[0]))
    flattened = gradients.reshape(-1, 3 * rows_brick * depth)
    references = brick_list.reshape(-1)
    slot_iota = jnp.arange(zone_count * slot_cap, dtype=jnp.int32)
    selector = (references[None, :] == slot_iota[:, None]).astype(jnp.float32)
    slot_grad = jnp.dot(selector, flattened, precision=lax.Precision.HIGHEST)
    slot_grad = slot_grad.reshape(zone_count, slot_cap, 3, rows_brick, depth)
    use_count = jnp.sum(selector, axis=1).reshape(zone_count, slot_cap)
    owned_iota = jnp.arange(owned_count, dtype=jnp.int32)
    owner_pick = (owner_list.reshape(-1)[None, :] == owned_iota[:, None]).astype(jnp.float32)
    returned, returned_uses = (
        lax.all_to_all(slot_grad, "zone", split_axis=0, concat_axis=0, tiled=True),
        lax.all_to_all(use_count, "zone", split_axis=0, concat_axis=0, tiled=True),
    )
    owned_grad = to_owned(returned, owner_pick).reshape(owned_count, 3, rows_brick, depth)
    intersection = jnp.dot(owner_pick, returned_uses.reshape(-1), precision=lax.Precision.HIGHEST)
    grad_total = lax.psum(owned_grad, "freq")
    descent = grad_total / (freq_count * jnp.maximum(intersection, 1.0))[:, None, None, None]
    return update(modulus, first_moment, second_moment, fiber, descent)


def solution(mesh):
    placed = (
        P("zone", None, None, None),
        P("zone", None, None, None),
        P("zone", None, None, None),
        P("zone", None, None),
        P("freq", "zone", None, None, None),
        P("freq"),
        P("zone", None, None),
        P("zone", None),
    )
    return jax.shard_map(
        on_device,
        mesh=mesh,
        in_specs=placed,
        out_specs=(
            P("zone", None, None, None),
            P("zone", None, None, None),
            P("zone", None, None, None),
        ),
        check_vma=False,
    )
```

profile of v0, /device:TPU:1, one launch (start us, length us, event | category | flops | bytes accessed | tf_op | source)
XLA Modules:
  0.0 472.6 jit_solution(13486487006673301540)
XLA Ops:
  11.8 18.5 %all-to-all-start = ((f32[32,2,4,1,1024]{4,2,1,3,0:T(4,128)}), f32[32,2,4,1,1024]{4,2,1,3,0:T(4,128)S(1)}, u32[]{:S(2)}, u32[]{:S(2)}) async-start(f32[32,2,4,1,1024]{4,2,1,3,0:T(4,128)} %broadcast_select_fusion), calls=%async_computation | async-start | bytes 2097152 | tf_op jit(solution)/shard_map/all_to_all | solution.py:75
  32.9 50.5 %all-to-all-done = f32[32,2,4,1,1024]{4,2,1,3,0:T(4,128)S(1)} async-done(((f32[32,2,4,1,1024]{4,2,1,3,0:T(4,128)}), f32[32,2,4,1,1024]{4,2,1,3,0:T(4,128)S(1)}, u32[]{:S(2)}, u32[]{:S(2)}) %all-to-all-start) | async-done | bytes 1048608 | tf_op jit(solution)/shard_map/all_to_all | solution.py:75
  83.4 7.2 %all-to-all-start.2 = ((f32[32,1,2]{2,1,0:T(1,128)}), f32[32,1,2]{2,1,0:T(1,128)S(1)}, u32[]{:S(2)}, u32[]{:S(2)}) async-start(f32[32,1,2]{2,1,0:T(1,128)} %bitcast.32), calls=%async_computation.2 | async-start | bytes 32768 | tf_op jit(solution)/shard_map/all_to_all | solution.py:98
  90.6 189.0 %while.12 = (s32[]{:T(128)}, f32[4,8,3,1,1024]{4,1,2,3,0:T(8,128)}, s32[4,8]{1,0:T(4,128)}, f32[64,4,1,1024]{3,1,0,2:T(4,128)S(1)}, f32[4,2,8,1024]{3,2,1,0:T(8,...) while((s32[]{:T(128)}, f32[4,8,3,1,1024]{4,1,2,3,0:T(8,128)}, s32[4,8]{1,0:T(4,128)}, ...), condition=%wide.region_7.8_spmd, body=%wide.region_0.7_spmd.sunk | while | flops 7111707 | bytes 32707772 | solution.py:86
  91.4 1.4 dynamic-slice_multiply_fusion.3
  123.0 1.4 fusion.211
  127.1 1.5 fusion.213
  128.6 1.6 unstack.190
  138.6 1.4 dynamic-slice_multiply_fusion.3
  170.3 1.4 fusion.211
  174.4 1.5 fusion.213
  175.8 1.6 unstack.190
  185.8 1.4 dynamic-slice_multiply_fusion.3
  221.6 1.5 fusion.213
  223.1 1.6 unstack.190
  233.1 1.4 dynamic-slice_multiply_fusion.3
  268.8 1.5 fusion.213
  270.3 1.6 unstack.190
  280.3 1.5 convolution_bitcast_fusion
  281.8 1.5 copy.104
  283.3 14.0 %all-to-all-start.1 = ((f32[32,2,3,1,1024]{4,1,3,2,0:T(2,128)}), f32[32,2,3,1,1024]{4,1,3,2,0:T(2,128)S(1)}, u32[]{:S(2)}, u32[]{:S(2)}) async-start(f32[32,2,3,1,1024]{4,1,3,2,0:T(2,128)} %copy.104), calls=%async_computation.1 | async-start | bytes 1572864 | tf_op jit(solution)/shard_map/all_to_all | solution.py:97
  299.4 39.1 %all-to-all-done.1 = f32[32,2,3,1,1024]{4,1,3,2,0:T(2,128)S(1)} async-done(((f32[32,2,3,1,1024]{4,1,3,2,0:T(2,128)}), f32[32,2,3,1,1024]{4,1,3,2,0:T(2,128)S(1)}, u32[]{:S(2)}, u32[]{:S(2)}) %all-to-all-start.1) | async-done | bytes 786464 | tf_op jit(solution)/shard_map/all_to_all | solution.py:97
  339.0 1.5 convolution_bitcast_fusion.1
  340.6 120.9 %all-reduce.72.cloned.1.call-done = f32[8,3,1,1024]{3,0,1,2:T(8,128)} async-done(((f32[8,3,1,1024]{3,0,1,2:T(8,128)}), f32[8,3,1,1024]{3,0,1,2:T(8,128)}) %all-reduce.72.cloned.1.call-update) | async-done | bytes 98320 | tf_op jit(solution)/shard_map/psum | solution.py:102
  (735 shorter events, 180.6 us)
Async XLA Ops:
  7.2 1.1 copy-start.33
  11.8 71.6 %all-to-all-start = ((f32[32,2,4,1,1024]{4,2,1,3,0:T(4,128)}), f32[32,2,4,1,1024]{4,2,1,3,0:T(4,128)S(1)}, u32[]{:S(2)}, u32[]{:S(2)}) async-start(f32[32,2,4,1,1024]{4,2,1,3,0:T(4,128)} %broadcast_select_fusion), calls=%async_computation | async-start | bytes 2097152 | tf_op jit(solution)/shard_map/all_to_all | solution.py:75
  83.4 199.9 %all-to-all-start.2 = ((f32[32,1,2]{2,1,0:T(1,128)}), f32[32,1,2]{2,1,0:T(1,128)S(1)}, u32[]{:S(2)}, u32[]{:S(2)}) async-start(f32[32,1,2]{2,1,0:T(1,128)} %bitcast.32), calls=%async_computation.2 | async-start | bytes 32768 | tf_op jit(solution)/shard_map/all_to_all | solution.py:98
  90.6 4.7 copy-start.30
  94.6 1.1 copy-start.1
  131.9 1.0 copy-start.6
  136.6 1.3 copy-start.31
  137.9 4.7 copy-start.30
  141.9 1.1 copy-start.1
  179.1 1.0 copy-start.6
  183.9 1.3 copy-start.31
  185.1 4.7 copy-start.30
  189.1 1.1 copy-start.1
  226.4 1.0 copy-start.6
  231.1 1.3 copy-start.31
  232.4 4.7 copy-start.30
  236.3 1.1 copy-start.1
  278.3 1.3 copy-start.31
  283.3 14.1 %copy-start.38 = (s32[1,32,2]{1,2,0:T(2,128)S(1)}, s32[1,32,2]{1,2,0:T(2,128)}, u32[]{:S(2)}) copy-start(s32[1,32,2]{1,2,0:T(2,128)} %param.16) | copy-start | bytes 772
  283.3 55.2 %all-to-all-start.1 = ((f32[32,2,3,1,1024]{4,1,3,2,0:T(2,128)}), f32[32,2,3,1,1024]{4,1,3,2,0:T(2,128)S(1)}, u32[]{:S(2)}, u32[]{:S(2)}) async-start(f32[32,2,3,1,1024]{4,1,3,2,0:T(2,128)} %copy.104), calls=%async_computation.1 | async-start | bytes 1572864 | tf_op jit(solution)/shard_map/all_to_all | solution.py:97
  297.3 164.2 %all-reduce.72.cloned.1.call-start = ((), (), s32[]{:S(2)}) async-start(), calls=%async_computation.3 | async-start | bytes 196608 | tf_op jit(solution)/shard_map/psum | solution.py:102
  339.0 122.5 %copy-start.35 = (f32[8,3,1,1024]{3,2,1,0:T(1,128)S(1)}, f32[8,3,1,1024]{3,2,1,0:T(1,128)}, u32[]{:S(2)}) copy-start(f32[8,3,1,1024]{3,2,1,0:T(1,128)} %param.11) | copy-start | bytes 294916
  339.0 122.5 %copy-start.36 = (f32[8,3,1,1024]{3,2,1,0:T(1,128)S(1)}, f32[8,3,1,1024]{3,2,1,0:T(1,128)}, u32[]{:S(2)}) copy-start(f32[8,3,1,1024]{3,2,1,0:T(1,128)} %param.12) | copy-start | bytes 294916
  340.5 121.1 %copy-start.32 = (f32[8,3,1,1024]{3,2,1,0:T(1,128)S(1)}, f32[8,3,1,1024]{3,2,1,0:T(1,128)}, u32[]{:S(2)}) copy-start(f32[8,3,1,1024]{3,2,1,0:T(1,128)} %param.10) | copy-start | bytes 294916
  (118 other events, 99.5 us)
Sparse Core Ops, SparseCore 0:
  340.6 120.8 all-reduce.71
where the time goes:
time: 476 us; the launch traced here: 473 us
  waiting for transfers between devices  211 us (44%)
  local copies, waits for them, and re-layouts  114 us (24%)
  other arithmetic  89.2 us (19%)
  starting transfers between devices  39.7 us (8%)
  between operations  14.2 us (3%)
    psum x1, waiting for transfers between devices, on_device(): grad_total = lax.psum(owned_grad, 'freq')  121 us
    all_to_all x1, waiting for transfers between devices, on_device(): lax.all_to_all(outgoing, 'zone', split_axis=0, concat_axis=0, tiled=True)  50.5 us
    all_to_all x1, waiting for transfers between devices, on_device(): lax.all_to_all(slot_grad, 'zone', split_axis=0, concat_axis=0, tiled=True)  39.1 us
    another operation x100, local copies, waits for them, and re-layouts, misfit(): jnp.stack([resid_real, resid_imag])  38.8 us
    another operation x20, other arithmetic, misfit(): jnp.stack([resid_real, resid_imag])  20.5 us
    all_to_all x1, starting transfers between devices, on_device(): lax.all_to_all(outgoing, 'zone', split_axis=0, concat_axis=0, tiled=True)  18.5 us
    squeeze x24, local copies, waits for them, and re-layouts, misfit(): stencil[0] - damping * stencil[1]  17.5 us
    squeeze x24, local copies, waits for them, and re-layouts, misfit(): stencil[1]  17.4 us
  transfers between devices with their start and end apart: 4, of which 3 were waited for; matrix products, arithmetic and copies ran while one was open for 38% of the time, Pallas kernels for 0%

commit v1 on v0

--- a/solution.py
+++ b/solution.py
@@ -99,7 +99,7 @@
     )
     owned_grad = to_owned(returned, owner_pick).reshape(owned_count, 3, rows_brick, depth)
     intersection = jnp.dot(owner_pick, returned_uses.reshape(-1), precision=lax.Precision.HIGHEST)
-    grad_total = lax.psum(owned_grad, "freq")
+    grad_total = jnp.sum(lax.all_gather(owned_grad, "freq"), axis=0)
     descent = grad_total / (freq_count * jnp.maximum(intersection, 1.0))[:, None, None, None]
     return update(modulus, first_moment, second_moment, fiber, descent)
 

time: 476 us -> 373 us (0.78)
  waiting for transfers between devices: 211 us -> 120 us
  local copies, waits for them, and re-layouts: 114 us -> 102 us
  starting transfers between devices: 39.7 us -> 33.4 us
  other arithmetic: 89.2 us -> 94.9 us
    psum x1 -> x0, waiting for transfers between devices: 121 us -> none  [on_device(): grad_total = lax.psum(owned_grad, 'freq')]
    all_to_all x1, waiting for transfers between devices: 0.01 us -> 13.4 us  [on_device(): lax.all_to_all(use_count, 'zone', split_axis=0, concat_axis=0, tiled=True)]
    while x260 -> x220, local copies, waits for them, and re-layouts: 13.7 us -> 0.51 us
    all_gather x0 -> x1, waiting for transfers between devices: none -> 12.5 us  [on_device(): grad_total = jnp.sum(lax.all_gather(owned_grad, 'freq'), axis=0)]
    mul x24, other arithmetic: 10.8 us -> 18.3 us  [misfit(): relax_rate * jnp.stack([resid_real, resid_imag]) / diagonal_term]
    all_to_all x1, starting transfers between devices: 14 us -> 7.01 us  [on_device(): lax.all_to_all(slot_grad, 'zone', split_axis=0, concat_axis=0, tiled=True)]
    gather x4, local copies, waits for them, and re-layouts: 2.5 us -> 7.4 us  [solve(): picked_rows = slot_data[brick_ids]]
  transfers between devices with their start and end apart: 4 -> 4, of which waited for: 3 -> 4; matrix products, arithmetic and copies ran while one was open for 38% -> 0% of each run, Pallas kernels for 0% -> 0%
where the time goes in v1:
time: 373 us; the launch traced here: 371 us
  waiting for transfers between devices  120 us (32%)
  local copies, waits for them, and re-layouts  102 us (27%)
  other arithmetic  94.9 us (25%)
  starting transfers between devices  33.4 us (9%)
  between operations  14.3 us (4%)
    all_to_all x1, waiting for transfers between devices, on_device(): lax.all_to_all(outgoing, 'zone', split_axis=0, concat_axis=0, tiled=True)  53 us
    all_to_all x1, waiting for transfers between devices, on_device(): lax.all_to_all(slot_grad, 'zone', split_axis=0, concat_axis=0, tiled=True)  41.2 us
    another operation x100, local copies, waits for them, and re-layouts, misfit(): jnp.stack([resid_real, resid_imag])  38.6 us
    another operation x20, other arithmetic, misfit(): jnp.stack([resid_real, resid_imag])  20.6 us
    all_to_all x1, starting transfers between devices, on_device(): lax.all_to_all(outgoing, 'zone', split_axis=0, concat_axis=0, tiled=True)  18.8 us
    mul x24, other arithmetic, misfit(): relax_rate * jnp.stack([resid_real, resid_imag]) / diagonal_term  18.3 us
    squeeze x24, local copies, waits for them, and re-layouts, misfit(): stencil[0] - damping * stencil[1]  17.4 us
    squeeze x24, local copies, waits for them, and re-layouts, misfit(): stencil[1]  17.3 us
  transfers between devices with their start and end apart: 4, of which 4 were waited for; matrix products, arithmetic and copies ran while one was open for 0% of the time, Pallas kernels for 0%

profile of v1, /device:TPU:1, one launch (start us, length us, event | category | flops | bytes accessed | tf_op | source)
XLA Modules:
  0.0 371.3 jit_solution(4326747618494390581)
XLA Ops:
  12.4 18.8 %all-to-all-start = ((f32[32,2,4,1,1024]{4,2,1,3,0:T(4,128)}), f32[32,2,4,1,1024]{4,2,1,3,0:T(4,128)}, u32[]{:S(2)}, u32[]{:S(2)}) async-start(f32[32,2,4,1,1024]{4,2,1,3,0:T(4,128)} %broadcast_select_fusion), calls=%async_computation | async-start | bytes 2097152 | tf_op jit(solution)/shard_map/all_to_all | solution.py:75
  31.2 53.0 %all-to-all-done = f32[32,2,4,1,1024]{4,2,1,3,0:T(4,128)} async-done(((f32[32,2,4,1,1024]{4,2,1,3,0:T(4,128)}), f32[32,2,4,1,1024]{4,2,1,3,0:T(4,128)}, u32[]{:S(2)}, u32[]{:S(2)}) %all-to-all-start) | async-done | bytes 1048608 | tf_op jit(solution)/shard_map/all_to_all | solution.py:75
  84.2 186.0 %while.12 = (s32[]{:T(128)}, f32[4,8,3,1,1024]{4,1,2,3,0:T(8,128)}, s32[4,8]{1,0:T(4,128)S(1)}, f32[64,4,1,1024]{3,1,0,2:T(4,128)}, f32[4,2,8,1024]{3,2,1,0:T(8,...) while((s32[]{:T(128)}, f32[4,8,3,1,1024]{4,1,2,3,0:T(8,128)}, s32[4,8]{1,0:T(4,128)S(1)}, ...), condition=%wide.region_7.8_spmd, body=%wide.region_0.7_spmd.sunk | while | flops 7111707 | bytes 23925808 | solution.py:86
  86.6 1.8 gather_fusion
  121.1 1.5 fusion.214
  122.6 1.7 unstack.190
  125.0 2.0 divide_multiply_fusion.17
  133.1 1.8 gather_fusion
  169.1 1.7 unstack.190
  171.5 2.0 divide_multiply_fusion.17
  179.6 1.8 gather_fusion
  215.6 1.7 unstack.190
  218.0 2.0 divide_multiply_fusion.17
  226.1 1.8 gather_fusion
  262.1 1.7 unstack.190
  264.5 2.0 divide_multiply_fusion.17
  270.2 1.5 convolution_bitcast_fusion
  271.7 1.5 copy.98
  273.2 7.0 %all-to-all-start.1 = ((f32[32,2,3,1,1024]{4,1,3,2,0:T(2,128)}), f32[32,2,3,1,1024]{4,1,3,2,0:T(2,128)S(1)}, u32[]{:S(2)}, u32[]{:S(2)}) async-start(f32[32,2,3,1,1024]{4,1,3,2,0:T(2,128)} %copy.98), calls=%async_computation.1 | async-start | bytes 1572864 | tf_op jit(solution)/shard_map/all_to_all | solution.py:97
  280.5 41.2 %all-to-all-done.1 = f32[32,2,3,1,1024]{4,1,3,2,0:T(2,128)S(1)} async-done(((f32[32,2,3,1,1024]{4,1,3,2,0:T(2,128)}), f32[32,2,3,1,1024]{4,1,3,2,0:T(2,128)S(1)}, u32[]{:S(2)}, u32[]{:S(2)}) %all-to-all-start.1) | async-done | bytes 786464 | tf_op jit(solution)/shard_map/all_to_all | solution.py:97
  324.4 7.6 %all-to-all-start.2 = ((f32[32,1,2]{2,1,0:T(1,128)}), f32[32,1,2]{2,1,0:T(1,128)S(1)}, u32[]{:S(2)}, u32[]{:S(2)}) async-start(f32[32,1,2]{2,1,0:T(1,128)} %bitcast.34), calls=%async_computation.2 | async-start | bytes 32768 | tf_op jit(solution)/shard_map/all_to_all | solution.py:98
  332.1 13.4 %all-to-all-done.2 = f32[32,1,2]{2,1,0:T(1,128)S(1)} async-done(((f32[32,1,2]{2,1,0:T(1,128)}), f32[32,1,2]{2,1,0:T(1,128)S(1)}, u32[]{:S(2)}, u32[]{:S(2)}) %all-to-all-start.2) | async-done | bytes 288 | tf_op jit(solution)/shard_map/all_to_all | solution.py:98
  347.0 12.5 %all-gather.3.cloned.1.call-done = f32[128,3,1024]{2,0,1:T(8,128)} async-done(((f32[8,3,1024]{2,0,1:T(8,128)}), f32[128,3,1024]{2,0,1:T(8,128)}) %all-gather.3.cloned.1.call-update) | async-done | bytes 1572880 | tf_op jit(solution)/shard_map/all_gather | solution.py:102
  359.5 1.5 bitcast_reduce_fusion
  (688 shorter events, 172.5 us)
Async XLA Ops:
  12.4 18.8 %copy-start.32 = (s32[4,8]{1,0:T(4,128)S(1)}, s32[4,8]{1,0:T(4,128)}, u32[]{:S(2)}) copy-start(s32[4,8]{1,0:T(4,128)} %param.17) | copy-start | bytes 388
  12.4 71.9 %all-to-all-start = ((f32[32,2,4,1,1024]{4,2,1,3,0:T(4,128)}), f32[32,2,4,1,1024]{4,2,1,3,0:T(4,128)}, u32[]{:S(2)}, u32[]{:S(2)}) async-start(f32[32,2,4,1,1024]{4,2,1,3,0:T(4,128)} %broadcast_select_fusion), calls=%async_computation | async-start | bytes 2097152 | tf_op jit(solution)/shard_map/all_to_all | solution.py:75
  88.7 1.3 copy-start.1
  122.6 4.4 %copy-start.3 = (f32[8,32,32]{2,1,0:T(8,128)S(1)}, f32[8,32,32]{2,1,0:T(8,128)}, u32[]{:S(2)}) copy-start(f32[8,32,32]{2,1,0:T(8,128)} %get-tuple-element.399) | copy-start | bytes 98308 | tf_op jit(solution)/shard_map/while
  127.4 1.2 copy-start.4
  127.9 1.5 copy-start.2
  135.2 1.3 copy-start.1
  169.1 4.4 %copy-start.3 = (f32[8,32,32]{2,1,0:T(8,128)S(1)}, f32[8,32,32]{2,1,0:T(8,128)}, u32[]{:S(2)}) copy-start(f32[8,32,32]{2,1,0:T(8,128)} %get-tuple-element.399) | copy-start | bytes 98308 | tf_op jit(solution)/shard_map/while
  174.4 1.5 copy-start.2
  181.7 1.3 copy-start.1
  215.6 4.4 %copy-start.3 = (f32[8,32,32]{2,1,0:T(8,128)S(1)}, f32[8,32,32]{2,1,0:T(8,128)}, u32[]{:S(2)}) copy-start(f32[8,32,32]{2,1,0:T(8,128)} %get-tuple-element.399) | copy-start | bytes 98308 | tf_op jit(solution)/shard_map/while
  220.4 1.2 copy-start.4
  220.9 1.5 copy-start.2
  228.2 1.3 copy-start.1
  262.1 4.4 %copy-start.3 = (f32[8,32,32]{2,1,0:T(8,128)S(1)}, f32[8,32,32]{2,1,0:T(8,128)}, u32[]{:S(2)}) copy-start(f32[8,32,32]{2,1,0:T(8,128)} %get-tuple-element.399) | copy-start | bytes 98308 | tf_op jit(solution)/shard_map/while
  267.4 1.5 copy-start.2
  271.7 8.6 %copy-start.31 = (s32[1,32,2]{1,2,0:T(2,128)S(1)}, s32[1,32,2]{1,2,0:T(2,128)}, u32[]{:S(2)}) copy-start(s32[1,32,2]{1,2,0:T(2,128)} %param.16) | copy-start | bytes 772
  273.2 48.5 %all-to-all-start.1 = ((f32[32,2,3,1,1024]{4,1,3,2,0:T(2,128)}), f32[32,2,3,1,1024]{4,1,3,2,0:T(2,128)S(1)}, u32[]{:S(2)}, u32[]{:S(2)}) async-start(f32[32,2,3,1,1024]{4,1,3,2,0:T(2,128)} %copy.98), calls=%async_computation.1 | async-start | bytes 1572864 | tf_op jit(solution)/shard_map/all_to_all | solution.py:97
  280.2 51.8 %copy-start.28 = (f32[8,1,1024]{2,1,0:T(1,128)S(1)}, f32[8,1,1024]{2,1,0:T(1,128)}, u32[]{:S(2)}) copy-start(f32[8,1,1024]{2,1,0:T(1,128)} %param.13) | copy-start | bytes 98308
  280.2 79.3 %all-gather.3.cloned.1.call-start = ((), (), s32[]{:S(2)}) async-start(), calls=%async_computation.3 | async-start | bytes 1671168 | tf_op jit(solution)/shard_map/all_gather | solution.py:102
  322.1 38.9 %copy-start.27 = (f32[8,3,1,1024]{3,2,1,0:T(1,128)S(1)}, f32[8,3,1,1024]{3,2,1,0:T(1,128)}, u32[]{:S(2)}) copy-start(f32[8,3,1,1024]{3,2,1,0:T(1,128)} %param.10) | copy-start | bytes 294916
  322.1 38.9 %copy-start.29 = (f32[8,3,1,1024]{3,2,1,0:T(1,128)S(1)}, f32[8,3,1,1024]{3,2,1,0:T(1,128)}, u32[]{:S(2)}) copy-start(f32[8,3,1,1024]{3,2,1,0:T(1,128)} %param.11) | copy-start | bytes 294916
  322.1 38.9 %copy-start.30 = (f32[8,3,1,1024]{3,2,1,0:T(1,128)S(1)}, f32[8,3,1,1024]{3,2,1,0:T(1,128)}, u32[]{:S(2)}) copy-start(f32[8,3,1,1024]{3,2,1,0:T(1,128)} %param.12) | copy-start | bytes 294916
  324.4 21.1 %all-to-all-start.2 = ((f32[32,1,2]{2,1,0:T(1,128)}), f32[32,1,2]{2,1,0:T(1,128)S(1)}, u32[]{:S(2)}, u32[]{:S(2)}) async-start(f32[32,1,2]{2,1,0:T(1,128)} %bitcast.34), calls=%async_computation.2 | async-start | bytes 32768 | tf_op jit(solution)/shard_map/all_to_all | solution.py:98
  (94 other events, 114.8 us)
Sparse Core Ops, SparseCore 0:
  323.8 35.7 all-gather.2
